TPU v7x, 32 devices: a whole 2x2x4 slice. The times are simulated.
32 devices in a mesh: island: 4 (over y, x), fsdp: 8 (over z, core).
Axes of the slice: x: 2, y: 2, z: 4, core: 2. Of those that a mesh axis runs over, the one named last changes fastest.
Arguments:
- tokens: bfloat16 [8192, 4096], P(('island', 'fsdp')), may hold values from -6 to 6
- upstream: bfloat16 [8192, 1024], P(('island', 'fsdp')), may hold values from -6 to 6
- params: float32 [4096, 1024], P('fsdp'), may hold values from -6 to 6
- momentum: float32 [4096, 1024], P('fsdp'), may hold values from -4 to 4
- projection: float32 [1024, 512], replicated, may hold values from -6 to 6
Outputs:
- values: bfloat16 [8192, 1024], P(('island', 'fsdp'))
- token_grads: bfloat16 [8192, 4096], P(('island', 'fsdp'))
- new_params: float32 [4096, 1024], P('fsdp')
- new_momentum: float32 [4096, 1024], P('fsdp')
All inputs are finite; a program needn't handle non-finite values.
Results may differ from a plain program's by a relative error of at most 0.012.
Values may be sent and summed in bfloat16 or wider, within the bound.
A program may use at most 128 MiB of HBM per device.

v0:
```python
import math

import jax
import jax.numpy as jnp
from jax import lax
from jax.sharding import PartitionSpec as P


def split_parts(matrix):
    high_part = matrix.astype(jnp.bfloat16)
    rest = matrix - lax.optimization_barrier(high_part).astype(jnp.float32)
    return (high_part, rest.astype(jnp.bfloat16))


def local(tokens, upstream, params, momentum, projection):
    half_weight = params.astype(jnp.bfloat16)
    inv_width = 1.0 / math.sqrt(tokens.shape[1])
    dims_feat = (((1,), (1,)), ((), ()))
    dims_rows = (((0,), (0,)), ((), ()))
    columns = tokens
    forward_sum = jnp.dot(
        columns,
        lax.all_gather(half_weight, "fsdp", axis=0, tiled=True),
        preferred_element_type=jnp.float32,
    )
    product = lax.dot_general(
        upstream,
        lax.all_gather(half_weight, "fsdp", axis=0, tiled=True),
        dims_feat,
        preferred_element_type=jnp.float32,
    )
    token_grads = (product * inv_width).astype(jnp.bfloat16)
    values = (forward_sum * inv_width).astype(jnp.bfloat16)
    fsdp_count = lax.axis_size("fsdp")
    scale_tok = 1.0 / math.sqrt(tokens.shape[0] * fsdp_count)
    proj_high, proj_low = split_parts(projection)
    sketch = jnp.dot(upstream, proj_high, preferred_element_type=jnp.float32) + jnp.dot(
        upstream, proj_low, preferred_element_type=jnp.float32
    )
    sketch_high, sketch_low = split_parts(sketch)
    columns = tokens
    first = lax.dot_general(columns, sketch_high, dims_rows, preferred_element_type=jnp.float32)
    second = lax.dot_general(columns, sketch_low, dims_rows, preferred_element_type=jnp.float32)
    compressed = (
        lax.psum_scatter(
            (first + second).astype(jnp.bfloat16), "fsdp", scatter_dimension=0, tiled=True
        ).astype(jnp.float32)
        * scale_tok
    )
    island_total = lax.psum(compressed.astype(jnp.bfloat16), "island").astype(jnp.float32)
    outer = jnp.dot(island_total, projection.T, precision=lax.Precision.HIGHEST) / (
        projection.shape[1] * lax.axis_size("island")
    )
    new_momentum = 0.9 * momentum + outer
    new_params = params - 0.7 * (outer + 0.9 * new_momentum)
    return (values, token_grads, new_params, new_momentum)


def solution(mesh):
    in_specs = (
        P(("island", "fsdp"), None),
        P(("island", "fsdp"), None),
        P("fsdp", None),
        P("fsdp", None),
        P(),
    )
    out_specs = (
        P(("island", "fsdp"), None),
        P(("island", "fsdp"), None),
        P("fsdp", None),
        P("fsdp", None),
    )
    return jax.shard_map(local, mesh=mesh, in_specs=in_specs, out_specs=out_specs, check_vma=False)
```

profile of v0, /device:TPU:0, one launch (start us, length us, event | category | flops | bytes accessed | tf_op | source)
XLA Modules:
  0.0 222.8 jit_solution(679768804462377622)
XLA Ops:
  7.2 0.0 copy-start
  7.2 0.0 copy-start.2
  7.2 0.0 reduce-scatter.2.cloned.1.call-start
  7.2 0.0 copy-start.1
  7.2 1.9 convert_element_type.43
  9.1 0.0 copy-done.2
  9.1 0.6 copy-done.1
  9.7 0.5 convolution_bitcast_fusion
  10.2 0.5 fusion.3
  10.7 0.0 copy-done
  10.7 1.3 fusion.4
  11.9 3.3 %fusion = bf16[4096,512]{0,1:T(8,128)(2,1)} fusion(f32[512,4096]{1,0:T(8,128)S(1)} %fusion.4, bf16[256,4096]{1,0:T(8,128)(2,1)S(1)} %copy-done, f32[256,512]{1,0:T(8,128)S(1)} %get-tuple-element.8, bf16[256,512]{1,0:T(8,128)(2,1)S(1)} %get-tuple-element.7), kind=kOutput, calls=%fused_computation.1 | convolution fusion | flops 1078329344 | bytes 15466496 | tf_op jit(solution)/shard_map/dot_general | solution.py:43
  15.3 0.0 reduce-scatter.2.cloned.1.call-update
  15.3 0.0 all-reduce.2.cloned.1.call-start
  15.4 52.8 %reduce-scatter.2.cloned.1.call-done = bf16[512,512]{0,1:T(8,128)(2,1)} async-done(((bf16[4096,512]{0,1:T(8,128)(2,1)}), bf16[512,512]{0,1:T(8,128)(2,1)}) %reduce-scatter.2.cloned.1.call-update) | async-done | bytes 524304 | tf_op jit(solution)/shard_map/reduce_scatter | solution.py:45
  68.2 1.9 multiply_convert_fusion
  70.1 0.0 all-reduce.2.cloned.1.call-update
  70.1 0.0 all-gather.2.cloned.1.call-start
  70.2 45.1 %all-reduce.2.cloned.1.call-done = bf16[512,512]{0,1:T(8,128)(2,1)} async-done(((bf16[512,512]{0,1:T(8,128)(2,1)}), bf16[512,512]{0,1:T(8,128)(2,1)}) %all-reduce.2.cloned.1.call-update) | async-done | bytes 524304 | tf_op jit(solution)/shard_map/psum | solution.py:50
  115.3 8.3 %multiply_subtract_fusion = (f32[512,1024]{1,0:T(8,128)}, f32[512,1024]{1,0:T(8,128)}, bf16[512,1024]{1,0:T(8,128)(2,1)}) fusion(f32[512,1024]{1,0:T(8,128)} %param.7, f32[512,1024]{1,0:T(8,128)} %param.8, bf16[512,512]{0,1:T(8,128)(2,1)} %all-reduce.2.cloned.1.call-done, f32[1024,512]{1,0:T(8,128)} %param.9), kind=kOutput, calls=%fused_computation.4 | convolution fusion | flops 3225419776 | bytes 12058624 | tf_op jit(solution)/shard_map/dot_general | solution.py:51
  123.6 0.0 all-gather.2.cloned.1.call-update
  123.6 82.2 %all-gather.2.cloned.1.call-done = bf16[4096,1024]{1,0:T(8,128)(2,1)} async-done(((bf16[512,1024]{1,0:T(8,128)(2,1)}), bf16[4096,1024]{1,0:T(8,128)(2,1)}) %all-gather.2.cloned.1.call-update) | async-done | bytes 8388624 | tf_op jit(solution)/shard_map/all_gather | solution.py:23
  205.8 0.0 copy-start.3
  205.8 6.7 %fusion.2 = bf16[256,1024]{1,0:T(8,128)(2,1)} fusion(bf16[256,4096]{1,0:T(8,128)(2,1)S(1)} %copy-done, bf16[4096,1024]{1,0:T(8,128)(2,1)} %all-gather.2.cloned.1.call-done), kind=kOutput, calls=%fused_computation.8 | convolution fusion | flops 2148007936 | bytes 11010048 | tf_op jit(solution)/shard_map/dot_general | solution.py:21
  212.5 0.0 copy-done.3
  212.5 3.8 %fusion.1 = bf16[256,4096]{1,0:T(8,128)(2,1)} fusion(bf16[256,1024]{1,0:T(8,128)(2,1)S(1)} %copy-done.2, bf16[4096,1024]{1,0:T(8,128)(2,1)S(1)} %copy-done.3), kind=kOutput, calls=%fused_computation.3 | convolution fusion | flops 2149580800 | bytes 11010048 | tf_op jit(solution)/shard_map/dot_general | solution.py:26
Async XLA Ops:
  7.2 3.5 %copy-start = (bf16[256,4096]{1,0:T(8,128)(2,1)S(1)}, bf16[256,4096]{1,0:T(8,128)(2,1)}, u32[]{:S(2)}) copy-start(bf16[256,4096]{1,0:T(8,128)(2,1)} %param.5) | copy-start | bytes 6291460
  7.2 2.0 copy-start.2
  7.2 61.0 %reduce-scatter.2.cloned.1.call-start = ((), (), s32[]{:S(2)}) async-start(), calls=%async_computation.2 | async-start | bytes 4718592 | tf_op jit(solution)/shard_map/reduce_scatter | solution.py:45
  7.2 2.5 %copy-start.1 = (f32[1024,512]{1,0:T(8,128)S(1)}, f32[1024,512]{1,0:T(8,128)}, u32[]{:S(2)}) copy-start(f32[1024,512]{1,0:T(8,128)} %param.9) | copy-start | bytes 6291460
  15.3 99.9 %all-reduce.2.cloned.1.call-start = ((), (), s32[]{:S(2)}) async-start(), calls=%async_computation.3 | async-start | bytes 1048576 | tf_op jit(solution)/shard_map/psum | solution.py:50
  70.1 135.7 %all-gather.2.cloned.1.call-start = ((), (), s32[]{:S(2)}) async-start(), calls=%async_computation.1 | async-start | bytes 9437184 | tf_op jit(solution)/shard_map/all_gather | solution.py:23
  205.8 6.7 %copy-start.3 = (bf16[4096,1024]{1,0:T(8,128)(2,1)S(1)}, bf16[4096,1024]{1,0:T(8,128)(2,1)}, u32[]{:S(2)}) copy-start(bf16[4096,1024]{1,0:T(8,128)(2,1)} %all-gather.2.cloned.1.call-done) | copy-start | bytes 25165828
Sparse Core Ops, SparseCore 0:
  15.4 52.6 reduce-scatter.1
  71.7 43.4 all-reduce.1
  123.7 82.0 all-gather.1
where the time goes:
time: 223 us
  waiting for transfers between devices  180 us (81%)
  matrix products  24.3 us (11%)
  between operations  13.8 us (6%)
  other arithmetic  3.8 us (2%)
    all_gather x1, waiting for transfers between devices, local(): lax.all_gather(half_weight, 'fsdp', axis=0, tiled=True)  82.2 us
    reduce_scatter x1, waiting for transfers between devices, local(): lax.psum_scatter((first + second).astype(jnp.bfloat16), 'fsdp', scatter_d...  52.8 us
    psum x1, waiting for transfers between devices, local(): lax.psum(compressed.astype(jnp.bfloat16), 'island').astype(jnp.float32)  45.1 us
    dot_general x1, matrix products, local(): jnp.dot(island_total, projection.T, precision=lax.Precision.HIGHEST)  8.35 us
    dot_general x1, matrix products, local(): jnp.dot(columns, lax.all_gather(half_weight, 'fsdp', axis=0, tiled=True),...  6.65 us
  transfers between devices with their start and end apart: 3, of which 3 were waited for; matrix products, arithmetic and copies ran while one was open for 0% of the time, Pallas kernels for 0%

commit v1 on v0

v1 whole, which is shorter than its diff:
```python
import functools
import math

import jax
import jax.numpy as jnp
from jax import lax
from jax.experimental import pallas as pl
from jax.experimental.pallas import tpu as pltpu
from jax.sharding import PartitionSpec as P

MESH = pl.DeviceIdType.MESH
F32 = jnp.float32
BF16 = jnp.bfloat16


def kernel(Z, I, tok_h, up_h, par_h, mom_h, proj_h, val_h, tg_h, np_h, nm_h,
           tok, up, par, mom, proj, projb, w, s, gsend, grecv, h, pb, zb, zr, fin, acc, val, tg, nm,
           in_sem, out_sem, tg_sem, np_sem, nm_sem,
           own_s, own_r, ag_s, ag_r, pl_s, pl_r, sib_s, sib_r, g_s, g_r, rp_s, rp_r, rz_s, rz_r, f_s, f_r):
    i = lax.axis_index("island")
    f = lax.axis_index("fsdp")
    z, c = f // 2, f % 2
    o = 1 - c
    sib = (i, z * 2 + o)
    R, KV = w.shape[1] * w.shape[2], w.shape[3]
    inv_width = 1.0 / math.sqrt(tok.shape[1])

    def zto(d):
        return lax.rem(z + d, Z)

    def zfrom(d):
        return lax.rem(z - d + Z, Z)

    def ito(e):
        return lax.rem(i + e, I)

    def ifrom(e):
        return lax.rem(i - e + I, I)

    ins = [pltpu.make_async_copy(a, b, in_sem.at[k]) for k, (a, b) in enumerate(
        ((par_h, par), (up_h, up), (proj_h, proj), (tok_h, tok), (mom_h, mom)))]
    for cp in ins:
        cp.start()

    barrier = pltpu.get_barrier_semaphore()
    for d in range(1, Z):
        pl.semaphore_signal(barrier, inc=1, device_id=(i, zto(d) * 2 + c), device_id_type=MESH)
    for e in range(1, I):
        pl.semaphore_signal(barrier, inc=1, device_id=(ito(e), f), device_id_type=MESH)
    pl.semaphore_signal(barrier, inc=1, device_id=sib, device_id_type=MESH)

    def remote(src, dst, ss, rs, to):
        return pltpu.make_async_remote_copy(src_ref=src, dst_ref=dst, send_sem=ss, recv_sem=rs, device_id=to, device_id_type=MESH)

    def c_own(fb):
        return remote(w.at[fb], w.at[fb], own_s, own_r, sib)

    def c_ag(d, fb, part):
        return remote(w.at[fb, part], w.at[fb, part], ag_s.at[d], ag_r.at[d], (i, zto(d) * 2 + c))

    def c_plane(e, d, fb, part):
        return remote(w.at[fb, part], w.at[fb, part], pl_s.at[e, d], pl_r.at[e, d], (ito(e), f))

    def c_sib(e, d, fb, part):
        return remote(w.at[fb, part], w.at[fb, part], sib_s.at[e, d], sib_r.at[e, d], sib)

    def c_g(d):
        return remote(gsend.at[d], grecv.at[d], g_s.at[d], g_r.at[d], sib)

    def c_rp(e, d):
        return remote(h.at[d, ito(e)], pb.at[e, d], rp_s.at[e, d], rp_r.at[e, d], (ito(e), f))

    def c_rz(d):
        return remote(zb.at[d], zr.at[d], rz_s.at[d], rz_r.at[d], (i, zto(d) * 2 + c))

    def c_fin(e, part):
        return remote(fin.at[part], fin.at[part], f_s.at[e], f_r.at[e], (ito(e), f))

    ins[0].wait()
    w[f] = par[...].astype(BF16)
    pl.semaphore_wait(barrier, Z + I - 1)
    for d in range(1, Z):
        c_ag(d, f, i).start()
    c_own(f).start()

    ins[1].wait()
    ins[2].wait()
    projb[...] = proj[...].astype(BF16)
    s[...] = jnp.dot(up[...], projb[...], preferred_element_type=F32).astype(BF16)
    ins[3].wait()

    def cols(fb):
        return pl.ds(pl.multiple_of(fb * R, R), R)

    def gblock(fb):
        return lax.dot_general(tok[:, cols(fb)], s[...], (((0,), (0,)), ((), ())), preferred_element_type=F32)

    def send_g(d, carry):
        gsend[d] = gblock(zto(d) * 2 + o).astype(BF16)
        c_g(d).start()
        return carry

    lax.fori_loop(0, Z, send_g, 0)

    def send_rp(d, carry):
        mine = gblock(zto(d) * 2 + c)
        c_g(d).wait_recv()
        h[d] = (mine + grecv[d].astype(F32)).astype(BF16).reshape(h.shape[1:])
        for e in range(1, I):
            c_rp(e, d).start()
        return carry

    lax.fori_loop(0, Z, send_rp, 0)

    acc[...] = jnp.zeros_like(acc)

    def c_tg(fb):
        return pltpu.make_async_copy(tg.at[fb], tg_h.at[:, cols(fb)], tg_sem.at[fb])

    def block(fb):
        wb = w[fb].reshape(R, KV)
        acc[...] += jnp.dot(tok[:, cols(fb)], wb, preferred_element_type=F32)
        product = lax.dot_general(up[...], wb, (((1,), (1,)), ((), ())), preferred_element_type=F32)
        tg[fb] = (product * inv_width).astype(BF16)
        c_tg(fb).start()

    def forward(d, carry):
        fb = zfrom(d) * 2 + c
        c_ag(d, fb, i).wait_recv()
        for e in range(1, I):
            c_plane(e, d, fb, i).start()
        c_sib(0, d, fb, i).start()
        return carry

    lax.fori_loop(1, Z, forward, 0)

    def send_rz(d, carry):
        total = h[d, i].astype(F32)
        for e in range(1, I):
            c_rp(e, d).wait_recv()
            total += pb[e, d].astype(F32)
        zb[d] = total.astype(BF16)

        @pl.when(d > 0)
        def _():
            c_rz(d).start()

        return carry

    lax.fori_loop(0, Z, send_rz, 0)

    block(f)
    c_own(z * 2 + o).wait_recv()
    block(z * 2 + o)

    total = zb[0].astype(F32)
    for d in range(1, Z):
        c_rz(d).wait_recv()
        total += zr[d].astype(F32)
    fin[i] = total.astype(BF16)
    for e in range(1, I):
        c_fin(e, i).start()

    factor = 1.0 / (math.sqrt(tok.shape[0] * 2 * Z) * projb.shape[1] * I)
    ins[4].wait()

    def out_np(part):
        return pltpu.make_async_copy(par.at[part], np_h.at[part], np_sem.at[part])

    def out_nm(part):
        return pltpu.make_async_copy(nm.at[part], nm_h.at[part], nm_sem.at[part])

    def finish(e, carry):
        part = ifrom(e)

        @pl.when(e > 0)
        def _():
            c_fin(e, part).wait_recv()

        outer = lax.dot_general(fin[part], projb[...], (((1,), (1,)), ((), ())), preferred_element_type=F32) * factor
        new_momentum = 0.9 * mom[part] + outer
        nm[part] = new_momentum
        par[part] = par[part] - 0.7 * (outer + 0.9 * new_momentum)
        out_np(part).start()
        out_nm(part).start()
        return carry

    def take(d, carry):
        fb = zfrom(d) * 2 + c
        for e in range(1, I):
            part = ifrom(e)
            c_plane(e, d, fb, part).wait_recv()
            c_sib(e, d, fb, part).start()
        block(fb)
        fo = zfrom(d) * 2 + o
        for e in range(I):
            c_sib(e, d, fo, ifrom(e)).wait_recv()
        block(fo)
        return carry

    lax.fori_loop(1, Z, take, 0)
    val[...] = (acc[...] * inv_width).astype(BF16)
    out_val = pltpu.make_async_copy(val, val_h, out_sem)
    out_val.start()
    lax.fori_loop(0, I, finish, 0)

    def drain_z(d, carry):
        fb = zfrom(d) * 2 + c
        c_ag(d, f, i).wait_send()
        c_rz(d).wait_send()
        c_sib(0, d, fb, i).wait_send()
        for e in range(1, I):
            c_plane(e, d, fb, i).wait_send()
            c_sib(e, d, fb, ifrom(e)).wait_send()
        return carry

    def drain_g(d, carry):
        c_g(d).wait_send()
        for e in range(1, I):
            c_rp(e, d).wait_send()
        return carry

    c_own(f).wait_send()
    lax.fori_loop(1, Z, drain_z, 0)
    lax.fori_loop(0, Z, drain_g, 0)
    for e in range(1, I):
        c_fin(e, i).wait_send()

    def drain_tg(k, carry):
        c_tg(k).wait()
        return carry

    lax.fori_loop(0, 2 * Z, drain_tg, 0)

    def drain_out(k, carry):
        out_np(k).wait()
        out_nm(k).wait()
        return carry

    lax.fori_loop(0, I, drain_out, 0)
    out_val.wait()


def local(Z, I, tokens, upstream, params, momentum, projection):
    T, D = tokens.shape
    R, KV = params.shape
    PR = projection.shape[1]
    q = R // I
    V = pltpu.VMEM
    dma = pltpu.SemaphoreType.DMA
    any_spec = pl.BlockSpec(memory_space=pl.ANY)
    outs = pl.pallas_call(
        functools.partial(kernel, Z, I),
        out_shape=(
            jax.ShapeDtypeStruct((T, KV), BF16),
            jax.ShapeDtypeStruct((T, D), BF16),
            jax.ShapeDtypeStruct((I, q, KV), F32),
            jax.ShapeDtypeStruct((I, q, KV), F32),
        ),
        in_specs=[any_spec] * 5,
        out_specs=(any_spec,) * 4,
        scratch_shapes=[
            V((T, D), BF16), V((T, KV), BF16), V((I, q, KV), F32), V((I, q, KV), F32), V((KV, PR), F32), V((KV, PR), BF16),
            V((2 * Z, I, q, KV), BF16), V((T, PR), BF16),
            V((Z, R, PR), BF16), V((Z, R, PR), BF16), V((Z, I, q, PR), BF16),
            V((I, Z, q, PR), BF16), V((Z, q, PR), BF16), V((Z, q, PR), BF16), V((I, q, PR), BF16),
            V((T, KV), F32), V((T, KV), BF16), V((2 * Z, T, R), BF16), V((I, q, KV), F32),
            dma((5,)), dma, dma((2 * Z,)), dma((I,)), dma((I,)),
            dma, dma, dma((Z,)), dma((Z,)), dma((I, Z)), dma((I, Z)), dma((I, Z)), dma((I, Z)),
            dma((Z,)), dma((Z,)), dma((I, Z)), dma((I, Z)), dma((Z,)), dma((Z,)), dma((I,)), dma((I,)),
        ],
        compiler_params=pltpu.CompilerParams(collective_id=0, has_side_effects=True, vmem_limit_bytes=56 * 2**20),
    )(tokens, upstream, params.reshape(I, q, KV), momentum.reshape(I, q, KV), projection)
    values, grads, new_params, new_momentum = outs
    return (values, grads, new_params.reshape(R, KV), new_momentum.reshape(R, KV))


def solution(mesh):
    I, F = mesh.shape["island"], mesh.shape["fsdp"]
    rows, shard, whole = P(("island", "fsdp"), None), P("fsdp", None), P()
    return jax.shard_map(
        functools.partial(local, F // 2, I), mesh=mesh,
        in_specs=(rows, rows, shard, shard, whole), out_specs=(rows, rows, shard, shard), check_vma=False,
    )
```

time: 223 us -> 85.5 us (0.38)
  waiting for transfers between devices: 180 us -> 0 us
  Pallas kernels: 0 us -> 75.9 us
  matrix products: 24.3 us -> 0 us
  between operations: 13.8 us -> 0.64 us
  local copies, waits for them, and re-layouts: 0.59 us -> 8.82 us
  other arithmetic: 3.8 us -> 0 us
    all_gather x1 -> x0, waiting for transfers between devices: 82.2 us -> none  [local(): lax.all_gather(half_weight, 'fsdp', axis=0, tiled=True)]
    pallas_call x0 -> x1, Pallas kernels: none -> 75.9 us  [local(): pl.pallas_call(functools.partial(kernel, Z, I), out_shape=(jax.ShapeDtype...]
    reduce_scatter x1 -> x0, waiting for transfers between devices: 52.8 us -> none  [local(): lax.psum_scatter((first + second).astype(jnp.bfloat16), 'fsdp', scatter_d...]
    psum x1 -> x0, waiting for transfers between devices: 45.1 us -> none  [local(): lax.psum(compressed.astype(jnp.bfloat16), 'island').astype(jnp.float32)]
    dot_general x7 -> x0, matrix products: 24.3 us -> none  [the longest x1 8.35 us: local(): jnp.dot(island_total, projection.T, precision=lax.Precision.HIGHEST)]
    unnamed x8, local copies, waits for them, and re-layouts: 0.59 us -> 8.82 us
    convert_element_type x2 -> x0, other arithmetic: 3.8 us -> none  [the longest x1 1.92 us: local(): compressed.astype(jnp.bfloat16)]
  transfers between devices with their start and end apart: 3 -> 0, of which waited for: 3 -> 0; matrix products, arithmetic and copies ran while one was open for 0% -> 0% of each run, Pallas kernels for 0% -> 0%
where the time goes in v1:
time: 85.5 us; the launch traced here: 85.3 us
  Pallas kernels  75.9 us (89%)
  local copies, waits for them, and re-layouts  8.82 us (10%)
    pallas_call x1, Pallas kernels, local(): pl.pallas_call(functools.partial(kernel, Z, I), out_shape=(jax.ShapeDtype...  75.9 us
    unnamed x8, local copies, waits for them, and re-layouts  8.82 us

profile of v1, /device:TPU:0, one launch (start us, length us, event | category | flops | bytes accessed | tf_op | source)
XLA Modules:
  0.0 85.3 jit_solution(5053587153726174428)
XLA Ops:
  0.6 75.9 %shard_map.84 = (bf16[256,1024]{1,0:T(8,128)(2,1)}, bf16[256,4096]{1,0:T(8,128)(2,1)}, f32[4,128,1024]{2,1,0:T(8,128)}, f32[4,128,1024]{2,1,0:T(8,128)}) custom-call(bf16[256,4096]{1,0:T(8,128)(2,1)} %tok_h.1, bf16[256,1024]{1,0:T(8,128)(2,1)} %up_h.1, f32[4,128,1024]{2,1,0:T(8,128)} %bitcast.4, f32[4,128,1024]{2,1,0:T(8,128)} %bitcast.5, f32[1024,512]{1,0:T(8,128)} %proj_h.1), custom_call_target="tpu_custom_call" | custom-call | tf_op jit(solution)/shard_map/pallas_call | solution.py:252
  76.5 1.9 %copy.13 = bf16[256,1024]{1,0:T(8,128)(2,1)} copy(bf16[256,1024]{1,0:T(8,128)(2,1)} %get-tuple-element.16) | data formatting | bytes 1048576
  78.4 0.0 copy-start.1
  78.4 3.3 %copy.14 = bf16[256,4096]{1,0:T(8,128)(2,1)} copy(bf16[256,4096]{1,0:T(8,128)(2,1)} %get-tuple-element.17) | data formatting | bytes 4194304
  81.7 0.0 copy-done.1
  81.7 0.0 copy-start
  81.7 1.3 %copy.15 = f32[512,1024]{1,0:T(8,128)} copy(f32[512,1024]{1,0:T(8,128)S(1)} %bitcast.7) | data formatting | bytes 4194304
  83.0 1.0 %copy-done = f32[4,128,1024]{2,1,0:T(8,128)S(1)} copy-done((f32[4,128,1024]{2,1,0:T(8,128)S(1)}, f32[4,128,1024]{2,1,0:T(8,128)}, u32[]{:S(2)}) %copy-start) | copy-done | bytes 2097176
  84.0 1.3 %copy.16 = f32[512,1024]{1,0:T(8,128)} copy(f32[512,1024]{1,0:T(8,128)S(1)} %bitcast.6) | data formatting | bytes 4194304
Async XLA Ops:
  78.4 3.3 %copy-start.1 = (f32[4,128,1024]{2,1,0:T(8,128)S(1)}, f32[4,128,1024]{2,1,0:T(8,128)}, u32[]{:S(2)}) copy-start(f32[4,128,1024]{2,1,0:T(8,128)} %get-tuple-element.10) | copy-start | bytes 6291460
  81.7 2.3 %copy-start = (f32[4,128,1024]{2,1,0:T(8,128)S(1)}, f32[4,128,1024]{2,1,0:T(8,128)}, u32[]{:S(2)}) copy-start(f32[4,128,1024]{2,1,0:T(8,128)} %get-tuple-element.11) | copy-start | bytes 6291460

commit v2 on v1

--- a/solution.py
+++ b/solution.py
@@ -16,7 +16,7 @@
 def kernel(Z, I, tok_h, up_h, par_h, mom_h, proj_h, val_h, tg_h, np_h, nm_h,
            tok, up, par, mom, proj, projb, w, s, gsend, grecv, h, pb, zb, zr, fin, acc, val, tg, nm,
            in_sem, out_sem, tg_sem, np_sem, nm_sem,
-           own_s, own_r, ag_s, ag_r, pl_s, pl_r, sib_s, sib_r, g_s, g_r, rp_s, rp_r, rz_s, rz_r, f_s, f_r):
+           own_s, own_r, ag_s, ag_r, pl_s, pl_r, sib_s, sib_r, agd_s, agd_r, sibd_s, sibd_r, pld_s, pld_r, sibl_s, sibl_r, g_s, g_r, rp_s, rp_r, rz_s, rz_r, f_s, f_r):
     i = lax.axis_index("island")
     f = lax.axis_index("fsdp")
     z, c = f // 2, f % 2
@@ -64,6 +64,23 @@
     def c_sib(e, d, fb, part):
         return remote(w.at[fb, part], w.at[fb, part], sib_s.at[e, d], sib_r.at[e, d], sib)
 
+    q = w.shape[2]
+    cut = q // 32 * 16
+    far = I - 1 - i
+    upper, lower = pl.ds(0, cut), pl.ds(cut, q - cut)
+
+    def c_agd(d, fb):
+        return remote(w.at[fb, far, upper], w.at[fb, far, upper], agd_s.at[d], agd_r.at[d], (i, zto(d) * 2 + c))
+
+    def c_sibd(d, fb, part):
+        return remote(w.at[fb, part, upper], w.at[fb, part, upper], sibd_s.at[d], sibd_r.at[d], sib)
+
+    def c_planed(d, fb, part):
+        return remote(w.at[fb, part, lower], w.at[fb, part, lower], pld_s.at[d], pld_r.at[d], (far, f))
+
+    def c_sibl(d, fb, part):
+        return remote(w.at[fb, part, lower], w.at[fb, part, lower], sibl_s.at[d], sibl_r.at[d], sib)
+
     def c_g(d):
         return remote(gsend.at[d], grecv.at[d], g_s.at[d], g_r.at[d], sib)
 
@@ -81,6 +98,9 @@
     pl.semaphore_wait(barrier, Z + I - 1)
     for d in range(1, Z):
         c_ag(d, f, i).start()
+    if cut:
+        for d in range(1, Z):
+            c_agd(d, f).start()
     c_own(f).start()
 
     ins[1].wait()
@@ -128,7 +148,11 @@
         fb = zfrom(d) * 2 + c
         c_ag(d, fb, i).wait_recv()
         for e in range(1, I):
-            c_plane(e, d, fb, i).start()
+            @pl.when(ito(e) != far)
+            def _():
+                c_plane(e, d, fb, i).start()
+
+        c_planed(d, fb, i).start()
         c_sib(0, d, fb, i).start()
         return carry
 
@@ -185,24 +209,45 @@
         out_nm(part).start()
         return carry
 
-    def take(d, carry):
+    def arrive(d):
         fb = zfrom(d) * 2 + c
-        for e in range(1, I):
-            part = ifrom(e)
-            c_plane(e, d, fb, part).wait_recv()
-            c_sib(e, d, fb, part).start()
-        block(fb)
+        if cut:
+            c_agd(d, fb).wait_recv()
+            c_sibd(d, fb, far).start()
+        for e in range(1, I):
+            @pl.when(ifrom(e) != far)
+            def _():
+                c_plane(e, d, fb, ifrom(e)).wait_recv()
+                c_sib(e, d, fb, ifrom(e)).start()
+
+        c_planed(d, fb, far).wait_recv()
+        c_sibl(d, fb, far).start()
+
+    def use(d):
+        block(zfrom(d) * 2 + c)
         fo = zfrom(d) * 2 + o
         for e in range(I):
-            c_sib(e, d, fo, ifrom(e)).wait_recv()
+            @pl.when(ifrom(e) != far)
+            def _():
+                c_sib(e, d, fo, ifrom(e)).wait_recv()
+
+        if cut:
+            c_sibd(d, fo, far).wait_recv()
+        c_sibl(d, fo, far).wait_recv()
         block(fo)
-        return carry
-
-    lax.fori_loop(1, Z, take, 0)
+
+    def take(d, carry):
+        arrive(d)
+        use(d)
+        return carry
+
+    lax.fori_loop(1, Z - 1, take, 0)
+    arrive(Z - 1)
+    lax.fori_loop(0, I, finish, 0)
+    use(Z - 1)
     val[...] = (acc[...] * inv_width).astype(BF16)
     out_val = pltpu.make_async_copy(val, val_h, out_sem)
     out_val.start()
-    lax.fori_loop(0, I, finish, 0)
 
     def drain_z(d, carry):
         fb = zfrom(d) * 2 + c
@@ -210,8 +255,19 @@
         c_rz(d).wait_send()
         c_sib(0, d, fb, i).wait_send()
         for e in range(1, I):
-            c_plane(e, d, fb, i).wait_send()
-            c_sib(e, d, fb, ifrom(e)).wait_send()
+            @pl.when(ito(e) != far)
+            def _():
+                c_plane(e, d, fb, i).wait_send()
+
+            @pl.when(ifrom(e) != far)
+            def _():
+                c_sib(e, d, fb, ifrom(e)).wait_send()
+
+        if cut:
+            c_agd(d, f).wait_send()
+            c_sibd(d, fb, far).wait_send()
+        c_planed(d, fb, i).wait_send()
+        c_sibl(d, fb, far).wait_send()
         return carry
 
     def drain_g(d, carry):
@@ -257,7 +313,7 @@
             jax.ShapeDtypeStruct((I, q, KV), F32),
             jax.ShapeDtypeStruct((I, q, KV), F32),
         ),
-        in_specs=[any_spec] * 5,
+        in_specs=[pl.BlockSpec(memory_space=pltpu.HBM)] * 5,
         out_specs=(any_spec,) * 4,
         scratch_shapes=[
             V((T, D), BF16), V((T, KV), BF16), V((I, q, KV), F32), V((I, q, KV), F32), V((KV, PR), F32), V((KV, PR), BF16),
@@ -267,9 +323,10 @@
             V((T, KV), F32), V((T, KV), BF16), V((2 * Z, T, R), BF16), V((I, q, KV), F32),
             dma((5,)), dma, dma((2 * Z,)), dma((I,)), dma((I,)),
             dma, dma, dma((Z,)), dma((Z,)), dma((I, Z)), dma((I, Z)), dma((I, Z)), dma((I, Z)),
+            *[dma((Z,))] * 8,
             dma((Z,)), dma((Z,)), dma((I, Z)), dma((I, Z)), dma((Z,)), dma((Z,)), dma((I,)), dma((I,)),
         ],
-        compiler_params=pltpu.CompilerParams(collective_id=0, has_side_effects=True, vmem_limit_bytes=56 * 2**20),
+        compiler_params=pltpu.CompilerParams(collective_id=0, has_side_effects=True, vmem_limit_bytes=46 * 2**20),
     )(tokens, upstream, params.reshape(I, q, KV), momentum.reshape(I, q, KV), projection)
     values, grads, new_params, new_momentum = outs
     return (values, grads, new_params.reshape(R, KV), new_momentum.reshape(R, KV))

time: 85.5 us -> 75.3 us (0.88)
  Pallas kernels: 75.9 us -> 68.7 us
  local copies, waits for them, and re-layouts: 8.82 us -> 5.79 us
    pallas_call x1, Pallas kernels: 75.9 us -> 68.7 us  [local(): pl.pallas_call(functools.partial(kernel, Z, I), out_shape=(jax.ShapeDtype...]
    unnamed x8 -> x6, local copies, waits for them, and re-layouts: 8.82 us -> 5.79 us
where the time goes in v2:
time: 75.3 us; the launch traced here: 75.1 us
  Pallas kernels  68.7 us (91%)
  local copies, waits for them, and re-layouts  5.79 us (8%)
    pallas_call x1, Pallas kernels, local(): pl.pallas_call(functools.partial(kernel, Z, I), out_shape=(jax.ShapeDtype...  68.7 us
    unnamed x6, local copies, waits for them, and re-layouts  5.79 us

profile of v2, /device:TPU:0, one launch (start us, length us, event | category | flops | bytes accessed | tf_op | source)
XLA Modules:
  0.0 75.1 jit_solution(15860317069455300523)
XLA Ops:
  0.6 0.0 copy-start
  0.6 1.0 %copy-done = bf16[256,1024]{1,0:T(8,128)(2,1)S(1)} copy-done((bf16[256,1024]{1,0:T(8,128)(2,1)S(1)}, bf16[256,1024]{1,0:T(8,128)(2,1)}, u32[]{:S(2)}) %copy-start) | copy-done | bytes 524312
  1.7 68.7 %shard_map.84 = (bf16[256,1024]{1,0:T(8,128)(2,1)S(1)}, bf16[256,4096]{1,0:T(8,128)(2,1)S(1)}, f32[4,128,1024]{2,1,0:T(8,128)S(1)}, f32[4,128,1024]{2,1,0:T(8,128)S(1)}) custom-call(bf16[256,4096]{1,0:T(8,128)(2,1)} %tok_h.1, bf16[256,1024]{1,0:T(8,128)(2,1)S(1)} %copy-done, f32[4,128,1024]{2,1,0:T(8,128)} %bitcast.6, f32[4,128,1024]{2,1,0:T(8,128)} %bitcast.7, ...), custom_call_target="tpu_custom_call" | custom-call | tf_op jit(solution)/shard_map/pallas_call | solution.py:308
  70.3 0.8 %copy.13 = bf16[256,1024]{1,0:T(8,128)(2,1)} copy(bf16[256,1024]{1,0:T(8,128)(2,1)S(1)} %get-tuple-element.16) | data formatting | bytes 1048576
  71.1 1.3 %copy.14 = bf16[256,4096]{1,0:T(8,128)(2,1)} copy(bf16[256,4096]{1,0:T(8,128)(2,1)S(1)} %get-tuple-element.17) | data formatting | bytes 4194304
  72.4 1.3 %copy.15 = f32[512,1024]{1,0:T(8,128)} copy(f32[512,1024]{1,0:T(8,128)S(1)} %bitcast.5) | data formatting | bytes 4194304
  73.8 1.3 %copy.16 = f32[512,1024]{1,0:T(8,128)} copy(f32[512,1024]{1,0:T(8,128)S(1)} %bitcast.4) | data formatting | bytes 4194304
Async XLA Ops:
  0.6 1.0 %copy-start = (bf16[256,1024]{1,0:T(8,128)(2,1)S(1)}, bf16[256,1024]{1,0:T(8,128)(2,1)}, u32[]{:S(2)}) copy-start(bf16[256,1024]{1,0:T(8,128)(2,1)} %up_h.1) | copy-start | bytes 1572868

commit v3 on v2

--- a/solution.py
+++ b/solution.py
@@ -39,7 +39,7 @@
 
     ins = [pltpu.make_async_copy(a, b, in_sem.at[k]) for k, (a, b) in enumerate(
         ((par_h, par), (up_h, up), (proj_h, proj), (tok_h, tok), (mom_h, mom)))]
-    for cp in ins:
+    for cp in ins[:4]:
         cp.start()
 
     barrier = pltpu.get_barrier_semaphore()
@@ -87,6 +87,28 @@
     def c_rp(e, d):
         return remote(h.at[d, ito(e)], pb.at[e, d], rp_s.at[e, d], rp_r.at[e, d], (ito(e), f))
 
+    two_stage = I == 4
+    beside, across = i + 1 - 2 * lax.rem(i, 2), lax.rem(i + 2, I)
+
+    def pair(d):
+        turn = lax.rem(d, 2) * (across - beside)
+        return beside + turn, across - turn
+
+    def c_r1(d, k):
+        first, _ = pair(d)
+        return remote(h.at[d, far if k else first], pb.at[1 + k, d], rp_s.at[1 + k, d], rp_r.at[1 + k, d], (first, f))
+
+    def c_r2(d):
+        _, second = pair(d)
+        return remote(h.at[d, second], pb.at[3, d], rp_s.at[3, d], rp_r.at[3, d], (second, f))
+
+    def stage2(d, carry):
+        _, second = pair(d)
+        c_r1(d, 1).wait_recv()
+        h[d, second] = (h[d, second].astype(F32) + pb[2, d].astype(F32)).astype(BF16)
+        c_r2(d).start()
+        return carry
+
     def c_rz(d):
         return remote(zb.at[d], zr.at[d], rz_s.at[d], rz_r.at[d], (i, zto(d) * 2 + c))
 
@@ -98,9 +120,6 @@
     pl.semaphore_wait(barrier, Z + I - 1)
     for d in range(1, Z):
         c_ag(d, f, i).start()
-    if cut:
-        for d in range(1, Z):
-            c_agd(d, f).start()
     c_own(f).start()
 
     ins[1].wait()
@@ -108,6 +127,7 @@
     projb[...] = proj[...].astype(BF16)
     s[...] = jnp.dot(up[...], projb[...], preferred_element_type=F32).astype(BF16)
     ins[3].wait()
+    ins[4].start()
 
     def cols(fb):
         return pl.ds(pl.multiple_of(fb * R, R), R)
@@ -115,22 +135,33 @@
     def gblock(fb):
         return lax.dot_general(tok[:, cols(fb)], s[...], (((0,), (0,)), ((), ())), preferred_element_type=F32)
 
-    def send_g(d, carry):
+    def send_g(d):
         gsend[d] = gblock(zto(d) * 2 + o).astype(BF16)
         c_g(d).start()
-        return carry
-
-    lax.fori_loop(0, Z, send_g, 0)
-
-    def send_rp(d, carry):
+
+    def send_rp(d):
         mine = gblock(zto(d) * 2 + c)
         c_g(d).wait_recv()
         h[d] = (mine + grecv[d].astype(F32)).astype(BF16).reshape(h.shape[1:])
-        for e in range(1, I):
-            c_rp(e, d).start()
-        return carry
-
-    lax.fori_loop(0, Z, send_rp, 0)
+        if two_stage:
+            c_r1(d, 1).start()
+            c_r1(d, 0).start()
+        else:
+            for e in range(1, I):
+                c_rp(e, d).start()
+
+    send_g(0)
+
+    def sketch(d, carry):
+        send_g(d)
+        send_rp(d - 1)
+        return carry
+
+    lax.fori_loop(1, Z, sketch, 0)
+    send_rp(Z - 1)
+    if cut:
+        for d in range(1, Z):
+            c_agd(d, f).start()
 
     acc[...] = jnp.zeros_like(acc)
 
@@ -156,13 +187,24 @@
         c_sib(0, d, fb, i).start()
         return carry
 
-    lax.fori_loop(1, Z, forward, 0)
+    if two_stage:
+        lax.fori_loop(0, Z // 2, stage2, 0)
+        lax.fori_loop(1, 2, forward, 0)
+        lax.fori_loop(Z // 2, Z, stage2, 0)
+        lax.fori_loop(2, Z, forward, 0)
+    else:
+        lax.fori_loop(1, Z, forward, 0)
 
     def send_rz(d, carry):
         total = h[d, i].astype(F32)
-        for e in range(1, I):
-            c_rp(e, d).wait_recv()
-            total += pb[e, d].astype(F32)
+        if two_stage:
+            c_r1(d, 0).wait_recv()
+            c_r2(d).wait_recv()
+            total += pb[1, d].astype(F32) + pb[3, d].astype(F32)
+        else:
+            for e in range(1, I):
+                c_rp(e, d).wait_recv()
+                total += pb[e, d].astype(F32)
         zb[d] = total.astype(BF16)
 
         @pl.when(d > 0)
@@ -272,8 +314,13 @@
 
     def drain_g(d, carry):
         c_g(d).wait_send()
-        for e in range(1, I):
-            c_rp(e, d).wait_send()
+        if two_stage:
+            c_r1(d, 0).wait_send()
+            c_r1(d, 1).wait_send()
+            c_r2(d).wait_send()
+        else:
+            for e in range(1, I):
+                c_rp(e, d).wait_send()
         return carry
 
     c_own(f).wait_send()

time: 75.3 us -> 70.6 us (0.938)
  Pallas kernels: 68.7 us -> 64 us
    pallas_call x1, Pallas kernels: 68.7 us -> 64 us  [local(): pl.pallas_call(functools.partial(kernel, Z, I), out_shape=(jax.ShapeDtype...]
where the time goes in v3:
time: 70.6 us; the launch traced here: 70.5 us
  Pallas kernels  64 us (91%)
  local copies, waits for them, and re-layouts  5.79 us (8%)
    pallas_call x1, Pallas kernels, local(): pl.pallas_call(functools.partial(kernel, Z, I), out_shape=(jax.ShapeDtype...  64 us
    unnamed x6, local copies, waits for them, and re-layouts  5.79 us

profile of v3, /device:TPU:0, one launch (start us, length us, event | category | flops | bytes accessed | tf_op | source)
XLA Modules:
  0.0 70.5 jit_solution(7456350545096835924)
XLA Ops:
  0.6 0.0 copy-start
  0.6 1.0 %copy-done = bf16[256,1024]{1,0:T(8,128)(2,1)S(1)} copy-done((bf16[256,1024]{1,0:T(8,128)(2,1)S(1)}, bf16[256,1024]{1,0:T(8,128)(2,1)}, u32[]{:S(2)}) %copy-start) | copy-done | bytes 524312
  1.7 64.0 %shard_map.84 = (bf16[256,1024]{1,0:T(8,128)(2,1)S(1)}, bf16[256,4096]{1,0:T(8,128)(2,1)S(1)}, f32[4,128,1024]{2,1,0:T(8,128)S(1)}, f32[4,128,1024]{2,1,0:T(8,128)S(1)}) custom-call(bf16[256,4096]{1,0:T(8,128)(2,1)} %tok_h.1, bf16[256,1024]{1,0:T(8,128)(2,1)S(1)} %copy-done, f32[4,128,1024]{2,1,0:T(8,128)} %bitcast.6, f32[4,128,1024]{2,1,0:T(8,128)} %bitcast.7, ...), custom_call_target="tpu_custom_call" | custom-call | tf_op jit(solution)/shard_map/pallas_call | solution.py:355
  65.7 0.8 %copy.13 = bf16[256,1024]{1,0:T(8,128)(2,1)} copy(bf16[256,1024]{1,0:T(8,128)(2,1)S(1)} %get-tuple-element.16) | data formatting | bytes 1048576
  66.5 1.3 %copy.14 = bf16[256,4096]{1,0:T(8,128)(2,1)} copy(bf16[256,4096]{1,0:T(8,128)(2,1)S(1)} %get-tuple-element.17) | data formatting | bytes 4194304
  67.8 1.3 %copy.15 = f32[512,1024]{1,0:T(8,128)} copy(f32[512,1024]{1,0:T(8,128)S(1)} %bitcast.5) | data formatting | bytes 4194304
  69.2 1.3 %copy.16 = f32[512,1024]{1,0:T(8,128)} copy(f32[512,1024]{1,0:T(8,128)S(1)} %bitcast.4) | data formatting | bytes 4194304
Async XLA Ops:
  0.6 1.0 %copy-start = (bf16[256,1024]{1,0:T(8,128)(2,1)S(1)}, bf16[256,1024]{1,0:T(8,128)(2,1)}, u32[]{:S(2)}) copy-start(bf16[256,1024]{1,0:T(8,128)(2,1)} %up_h.1) | copy-start | bytes 1572868

commit v4 on v3

--- a/solution.py
+++ b/solution.py
@@ -55,8 +55,28 @@
     def c_own(fb):
         return remote(w.at[fb], w.at[fb], own_s, own_r, sib)
 
-    def c_ag(d, fb, part):
-        return remote(w.at[fb, part], w.at[fb, part], ag_s.at[d], ag_r.at[d], (i, zto(d) * 2 + c))
+    def c_ag(down, d, fb):
+        to = lax.rem(z + (Z - 1 if down else 1), Z)
+        return remote(w.at[fb, i], w.at[fb, i], ag_s.at[down * Z + d], ag_r.at[d], (i, to * 2 + c))
+
+    def ag_own(act):
+        @pl.when(z < Z - 1)
+        def _():
+            act(c_ag(0, 1, f))
+
+        @pl.when(z > 0)
+        def _():
+            act(c_ag(1, Z - 1, f))
+
+    def ag_relay_up(d, act):
+        @pl.when(z < Z - 1)
+        def _():
+            act(c_ag(0, d + 1, zfrom(d) * 2 + c))
+
+    def ag_relay_down(d, act):
+        @pl.when(z > 0)
+        def _():
+            act(c_ag(1, d - 1, zfrom(d) * 2 + c))
 
     def c_plane(e, d, fb, part):
         return remote(w.at[fb, part], w.at[fb, part], pl_s.at[e, d], pl_r.at[e, d], (ito(e), f))
@@ -118,8 +138,7 @@
     ins[0].wait()
     w[f] = par[...].astype(BF16)
     pl.semaphore_wait(barrier, Z + I - 1)
-    for d in range(1, Z):
-        c_ag(d, f, i).start()
+    ag_own(lambda copy: copy.start())
     c_own(f).start()
 
     ins[1].wait()
@@ -159,10 +178,6 @@
 
     lax.fori_loop(1, Z, sketch, 0)
     send_rp(Z - 1)
-    if cut:
-        for d in range(1, Z):
-            c_agd(d, f).start()
-
     acc[...] = jnp.zeros_like(acc)
 
     def c_tg(fb):
@@ -175,9 +190,10 @@
         tg[fb] = (product * inv_width).astype(BF16)
         c_tg(fb).start()
 
-    def forward(d, carry):
+    def forward(d, up):
         fb = zfrom(d) * 2 + c
-        c_ag(d, fb, i).wait_recv()
+        c_ag(0 if up else 1, d, fb).wait_recv()
+        (ag_relay_up if up else ag_relay_down)(d, lambda copy: copy.start())
         for e in range(1, I):
             @pl.when(ito(e) != far)
             def _():
@@ -185,15 +201,27 @@
 
         c_planed(d, fb, i).start()
         c_sib(0, d, fb, i).start()
-        return carry
-
+
+    def hop(k, carry):
+        @pl.when(z >= k)
+        def _():
+            forward(k, True)
+
+        @pl.when(z + k < Z)
+        def _():
+            forward(Z - k, False)
+
+        return carry
+
+    lax.fori_loop(1, 2, hop, 0)
     if two_stage:
         lax.fori_loop(0, Z // 2, stage2, 0)
-        lax.fori_loop(1, 2, forward, 0)
+    lax.fori_loop(2, Z - 1, hop, 0)
+    if cut:
+        c_agd(1, f).start()
+    if two_stage:
         lax.fori_loop(Z // 2, Z, stage2, 0)
-        lax.fori_loop(2, Z, forward, 0)
-    else:
-        lax.fori_loop(1, Z, forward, 0)
+    lax.fori_loop(max(2, Z - 1), Z, hop, 0)
 
     def send_rz(d, carry):
         total = h[d, i].astype(F32)
@@ -214,6 +242,9 @@
         return carry
 
     lax.fori_loop(0, Z, send_rz, 0)
+    if cut:
+        for d in range(2, Z):
+            c_agd(d, f).start()
 
     block(f)
     c_own(z * 2 + o).wait_recv()
@@ -293,7 +324,14 @@
 
     def drain_z(d, carry):
         fb = zfrom(d) * 2 + c
-        c_ag(d, f, i).wait_send()
+        @pl.when(z >= d)
+        def _():
+            ag_relay_up(d, lambda copy: copy.wait_send())
+
+        @pl.when(z < d)
+        def _():
+            ag_relay_down(d, lambda copy: copy.wait_send())
+
         c_rz(d).wait_send()
         c_sib(0, d, fb, i).wait_send()
         for e in range(1, I):
@@ -324,6 +362,7 @@
         return carry
 
     c_own(f).wait_send()
+    ag_own(lambda copy: copy.wait_send())
     lax.fori_loop(1, Z, drain_z, 0)
     lax.fori_loop(0, Z, drain_g, 0)
     for e in range(1, I):
@@ -369,7 +408,7 @@
             V((I, Z, q, PR), BF16), V((Z, q, PR), BF16), V((Z, q, PR), BF16), V((I, q, PR), BF16),
             V((T, KV), F32), V((T, KV), BF16), V((2 * Z, T, R), BF16), V((I, q, KV), F32),
             dma((5,)), dma, dma((2 * Z,)), dma((I,)), dma((I,)),
-            dma, dma, dma((Z,)), dma((Z,)), dma((I, Z)), dma((I, Z)), dma((I, Z)), dma((I, Z)),
+            dma, dma, dma((2 * Z,)), dma((Z,)), dma((I, Z)), dma((I, Z)), dma((I, Z)), dma((I, Z)),
             *[dma((Z,))] * 8,
             dma((Z,)), dma((Z,)), dma((I, Z)), dma((I, Z)), dma((Z,)), dma((Z,)), dma((I,)), dma((I,)),
         ],

time: 70.6 us -> 80.4 us (1.14)
  Pallas kernels: 64 us -> 73.8 us
    pallas_call x1, Pallas kernels: 64 us -> 73.8 us  [local(): pl.pallas_call(functools.partial(kernel, Z, I), out_shape=(jax.ShapeDtype...]
where the time goes in v4:
time: 80.4 us; the launch traced here: 80.2 us
  Pallas kernels  73.8 us (92%)
  local copies, waits for them, and re-layouts  5.79 us (7%)
    pallas_call x1, Pallas kernels, local(): pl.pallas_call(functools.partial(kernel, Z, I), out_shape=(jax.ShapeDtype...  73.8 us
    unnamed x6, local copies, waits for them, and re-layouts  5.79 us

profile of v4, /device:TPU:0, one launch (start us, length us, event | category | flops | bytes accessed | tf_op | source)
XLA Modules:
  0.0 80.2 jit_solution(14495543531805294341)
XLA Ops:
  0.6 0.0 copy-start
  0.6 1.0 %copy-done = bf16[256,1024]{1,0:T(8,128)(2,1)S(1)} copy-done((bf16[256,1024]{1,0:T(8,128)(2,1)S(1)}, bf16[256,1024]{1,0:T(8,128)(2,1)}, u32[]{:S(2)}) %copy-start) | copy-done | bytes 524312
  1.7 73.8 %shard_map.84 = (bf16[256,1024]{1,0:T(8,128)(2,1)S(1)}, bf16[256,4096]{1,0:T(8,128)(2,1)S(1)}, f32[4,128,1024]{2,1,0:T(8,128)S(1)}, f32[4,128,1024]{2,1,0:T(8,128)S(1)}) custom-call(bf16[256,4096]{1,0:T(8,128)(2,1)} %tok_h.1, bf16[256,1024]{1,0:T(8,128)(2,1)S(1)} %copy-done, f32[4,128,1024]{2,1,0:T(8,128)} %bitcast.6, f32[4,128,1024]{2,1,0:T(8,128)} %bitcast.7, ...), custom_call_target="tpu_custom_call" | custom-call | tf_op jit(solution)/shard_map/pallas_call | solution.py:394
  75.4 0.8 copy.13
  76.2 1.3 %copy.14 = bf16[256,4096]{1,0:T(8,128)(2,1)} copy(bf16[256,4096]{1,0:T(8,128)(2,1)S(1)} %get-tuple-element.17) | data formatting | bytes 4194304
  77.6 1.3 %copy.15 = f32[512,1024]{1,0:T(8,128)} copy(f32[512,1024]{1,0:T(8,128)S(1)} %bitcast.5) | data formatting | bytes 4194304
  78.9 1.3 %copy.16 = f32[512,1024]{1,0:T(8,128)} copy(f32[512,1024]{1,0:T(8,128)S(1)} %bitcast.4) | data formatting | bytes 4194304
Async XLA Ops:
  0.6 1.0 %copy-start = (bf16[256,1024]{1,0:T(8,128)(2,1)S(1)}, bf16[256,1024]{1,0:T(8,128)(2,1)}, u32[]{:S(2)}) copy-start(bf16[256,1024]{1,0:T(8,128)(2,1)} %up_h.1) | copy-start | bytes 1572868

commit v5 on v3

--- a/solution.py
+++ b/solution.py
@@ -215,9 +215,65 @@
 
     lax.fori_loop(0, Z, send_rz, 0)
 
+    factor = 1.0 / (math.sqrt(tok.shape[0] * 2 * Z) * projb.shape[1] * I)
+    ins[4].wait()
+
+    def out_np(part):
+        return pltpu.make_async_copy(par.at[part], np_h.at[part], np_sem.at[part])
+
+    def out_nm(part):
+        return pltpu.make_async_copy(nm.at[part], nm_h.at[part], nm_sem.at[part])
+
+    def finish(e, carry):
+        part = ifrom(e)
+
+        @pl.when(e > 0)
+        def _():
+            c_fin(e, part).wait_recv()
+
+        outer = lax.dot_general(fin[part], projb[...], (((1,), (1,)), ((), ())), preferred_element_type=F32) * factor
+        new_momentum = 0.9 * mom[part] + outer
+        nm[part] = new_momentum
+        par[part] = par[part] - 0.7 * (outer + 0.9 * new_momentum)
+        out_np(part).start()
+        out_nm(part).start()
+        return carry
+
+    def arrive(d):
+        fb = zfrom(d) * 2 + c
+        for e in range(1, I):
+            @pl.when(ifrom(e) != far)
+            def _():
+                c_plane(e, d, fb, ifrom(e)).wait_recv()
+                c_sib(e, d, fb, ifrom(e)).start()
+
+        c_planed(d, fb, far).wait_recv()
+        c_sibl(d, fb, far).start()
+
+    def arrive_far(d):
+        if cut:
+            fb = zfrom(d) * 2 + c
+            c_agd(d, fb).wait_recv()
+            c_sibd(d, fb, far).start()
+
+    def use(d):
+        block(zfrom(d) * 2 + c)
+        fo = zfrom(d) * 2 + o
+        for e in range(I):
+            @pl.when(ifrom(e) != far)
+            def _():
+                c_sib(e, d, fo, ifrom(e)).wait_recv()
+
+        if cut:
+            c_sibd(d, fo, far).wait_recv()
+        c_sibl(d, fo, far).wait_recv()
+        block(fo)
+
     block(f)
     c_own(z * 2 + o).wait_recv()
     block(z * 2 + o)
+
+    arrive(1)
 
     total = zb[0].astype(F32)
     for d in range(1, Z):
@@ -227,64 +283,14 @@
     for e in range(1, I):
         c_fin(e, i).start()
 
-    factor = 1.0 / (math.sqrt(tok.shape[0] * 2 * Z) * projb.shape[1] * I)
-    ins[4].wait()
-
-    def out_np(part):
-        return pltpu.make_async_copy(par.at[part], np_h.at[part], np_sem.at[part])
-
-    def out_nm(part):
-        return pltpu.make_async_copy(nm.at[part], nm_h.at[part], nm_sem.at[part])
-
-    def finish(e, carry):
-        part = ifrom(e)
-
-        @pl.when(e > 0)
-        def _():
-            c_fin(e, part).wait_recv()
-
-        outer = lax.dot_general(fin[part], projb[...], (((1,), (1,)), ((), ())), preferred_element_type=F32) * factor
-        new_momentum = 0.9 * mom[part] + outer
-        nm[part] = new_momentum
-        par[part] = par[part] - 0.7 * (outer + 0.9 * new_momentum)
-        out_np(part).start()
-        out_nm(part).start()
-        return carry
-
-    def arrive(d):
-        fb = zfrom(d) * 2 + c
-        if cut:
-            c_agd(d, fb).wait_recv()
-            c_sibd(d, fb, far).start()
-        for e in range(1, I):
-            @pl.when(ifrom(e) != far)
-            def _():
-                c_plane(e, d, fb, ifrom(e)).wait_recv()
-                c_sib(e, d, fb, ifrom(e)).start()
-
-        c_planed(d, fb, far).wait_recv()
-        c_sibl(d, fb, far).start()
-
-    def use(d):
-        block(zfrom(d) * 2 + c)
-        fo = zfrom(d) * 2 + o
-        for e in range(I):
-            @pl.when(ifrom(e) != far)
-            def _():
-                c_sib(e, d, fo, ifrom(e)).wait_recv()
-
-        if cut:
-            c_sibd(d, fo, far).wait_recv()
-        c_sibl(d, fo, far).wait_recv()
-        block(fo)
-
     def take(d, carry):
-        arrive(d)
+        arrive_far(d)
+        arrive(d + 1)
         use(d)
         return carry
 
     lax.fori_loop(1, Z - 1, take, 0)
-    arrive(Z - 1)
+    arrive_far(Z - 1)
     lax.fori_loop(0, I, finish, 0)
     use(Z - 1)
     val[...] = (acc[...] * inv_width).astype(BF16)

time: 70.6 us -> 70.6 us (level)
  no operation moved by 1% of the time
where the time goes in v5:
time: 70.6 us; the launch traced here: 70.5 us
  Pallas kernels  64 us (91%)
  local copies, waits for them, and re-layouts  5.79 us (8%)
    pallas_call x1, Pallas kernels, local(): pl.pallas_call(functools.partial(kernel, Z, I), out_shape=(jax.ShapeDtype...  64 us
    unnamed x6, local copies, waits for them, and re-layouts  5.79 us

profile of v5, /device:TPU:0, one launch (start us, length us, event | category | flops | bytes accessed | tf_op | source)
XLA Modules:
  0.0 70.5 jit_solution(12481053359637282283)
XLA Ops:
  0.6 0.0 copy-start
  0.6 1.0 %copy-done = bf16[256,1024]{1,0:T(8,128)(2,1)S(1)} copy-done((bf16[256,1024]{1,0:T(8,128)(2,1)S(1)}, bf16[256,1024]{1,0:T(8,128)(2,1)}, u32[]{:S(2)}) %copy-start) | copy-done | bytes 524312
  1.7 64.0 %shard_map.84 = (bf16[256,1024]{1,0:T(8,128)(2,1)S(1)}, bf16[256,4096]{1,0:T(8,128)(2,1)S(1)}, f32[4,128,1024]{2,1,0:T(8,128)S(1)}, f32[4,128,1024]{2,1,0:T(8,128)S(1)}) custom-call(bf16[256,4096]{1,0:T(8,128)(2,1)} %tok_h.1, bf16[256,1024]{1,0:T(8,128)(2,1)S(1)} %copy-done, f32[4,128,1024]{2,1,0:T(8,128)} %bitcast.6, f32[4,128,1024]{2,1,0:T(8,128)} %bitcast.7, ...), custom_call_target="tpu_custom_call" | custom-call | tf_op jit(solution)/shard_map/pallas_call | solution.py:361
  65.7 0.8 %copy.13 = bf16[256,1024]{1,0:T(8,128)(2,1)} copy(bf16[256,1024]{1,0:T(8,128)(2,1)S(1)} %get-tuple-element.16) | data formatting | bytes 1048576
  66.5 1.3 %copy.14 = bf16[256,4096]{1,0:T(8,128)(2,1)} copy(bf16[256,4096]{1,0:T(8,128)(2,1)S(1)} %get-tuple-element.17) | data formatting | bytes 4194304
  67.8 1.3 %copy.15 = f32[512,1024]{1,0:T(8,128)} copy(f32[512,1024]{1,0:T(8,128)S(1)} %bitcast.5) | data formatting | bytes 4194304
  69.2 1.3 %copy.16 = f32[512,1024]{1,0:T(8,128)} copy(f32[512,1024]{1,0:T(8,128)S(1)} %bitcast.4) | data formatting | bytes 4194304
Async XLA Ops:
  0.6 1.0 %copy-start = (bf16[256,1024]{1,0:T(8,128)(2,1)S(1)}, bf16[256,1024]{1,0:T(8,128)(2,1)}, u32[]{:S(2)}) copy-start(bf16[256,1024]{1,0:T(8,128)(2,1)} %up_h.1) | copy-start | bytes 1572868
